TPU v7x, 32 devices: a whole 2x2x4 slice. The times are simulated.
32 devices in a mesh: groups: 2 (over y), seq: 16 (over z, x, core).
Axes of the slice: x: 2, y: 2, z: 4, core: 2. Of those that a mesh axis runs over, the one named last changes fastest.
Arguments:
- query_src: bfloat16 [4096, 2048], P(('groups', 'seq')), parts along dimension 0, may hold values from -6 to 6
- key_src: bfloat16 [4096, 2048], P(('groups', 'seq')), parts along dimension 0, may hold values from -6 to 6
- value_src: bfloat16 [4096, 2048], P(('groups', 'seq')), parts along dimension 0, may hold values from -6 to 6
- up_query: bfloat16 [4096, 2048], P(('groups', 'seq')), parts along dimension 0, may hold values from -6 to 6
- query_gain: float32 [2048], replicated, may hold values from 1.2 to 2.4
- key_gain: float32 [2048], replicated, may hold values from 1.2 to 2.4
- up_gain: float32 [2048], replicated, may hold values from 1.5 to 5
Outputs:
- upsampled: bfloat16 [4096, 2048], P(('groups', 'seq')), parts along dimension 0
There are 2 independent parts, one for each index of `groups`. A program takes and returns all parts, laid end to end along the dimension named above; an argument that names none is the same for every part. Nothing has to cross between parts.
All inputs are finite; a program needn't handle non-finite values.
Results may differ from a plain program's by a relative error of at most 0.002.
The roundings to bfloat16 on the way count: a program that leaves them out, or rounds other values in their place, can miss the bound.
Values may be sent and summed in bfloat16 or wider, within the bound.
A program may use at most 128 MiB of HBM per device.

v0:
```python
import math

import jax
import jax.numpy as jnp
from jax import lax
from jax.sharding import PartitionSpec as P

HEADS = 16
HDIM = 128
SHORT = 4
SHIFT = 3


epsilon = 1e-06


def shifted(value, axis, steps):
    count = lax.axis_size(axis)
    leading, last = (max(0, -steps), min(count, count - steps))
    return lax.ppermute(value, axis, [(source, source + steps) for source in range(leading, last)])


def head_norm(values, gain_vector):
    row_count = values.shape[0]
    by_head = values.reshape(row_count, HEADS, HDIM)
    inverse_rms = lax.rsqrt(jnp.mean(by_head * by_head, axis=2, keepdims=True) + epsilon)
    return (by_head * inverse_rms * gain_vector.reshape(1, HEADS, HDIM)).reshape(
        row_count, HEADS * HDIM
    )


def row_norm(values):
    return values * lax.rsqrt(jnp.mean(values * values, axis=-1, keepdims=True) + epsilon)


def pooled_rows(source, edge_rows):
    widened = jnp.concatenate([edge_rows, source[: source.shape[0] - SHIFT]], axis=0).astype(
        jnp.float32
    )
    return jnp.mean(widened.reshape(-1, SHORT, widened.shape[1]), axis=1)


def blocked_attention(queries, query_limit, key_rows, value_rows, key_positions, block_size):
    head_count, query_count, head_size = queries.shape
    block_total = key_rows.shape[1] // block_size
    ceiling = jnp.max(query_limit)

    def visit_block(block_index, totals):
        offset = block_index * block_size
        block_pos = lax.dynamic_slice_in_dim(key_positions, offset, block_size, 0)

        def compute(state):
            numer_in, denom_in = state
            key_block = lax.dynamic_slice_in_dim(key_rows, offset, block_size, 1)
            value_block = lax.dynamic_slice_in_dim(value_rows, offset, block_size, 1)
            scores = jnp.einsum(
                "hqd,hkd->hqk", queries, key_block, preferred_element_type=jnp.float32
            ) / math.sqrt(HDIM)
            visible = block_pos[None, :] <= query_limit[:, None]
            exponent = jnp.where(visible[None], jnp.exp(scores), 0.0)
            denom_out = denom_in + jnp.sum(exponent, axis=2)
            numer_out = numer_in + jnp.einsum(
                "hqk,hkd->hqd",
                exponent.astype(jnp.bfloat16),
                value_block,
                preferred_element_type=jnp.float32,
            )
            return (numer_out, denom_out)

        return lax.cond(jnp.min(block_pos) <= ceiling, compute, lambda state: state, totals)

    initial = (
        jnp.zeros((head_count, query_count, head_size), jnp.float32),
        jnp.zeros((head_count, query_count), jnp.float32),
    )
    numerator, denominator = lax.fori_loop(0, block_total, visit_block, initial)
    return numerator / denominator[:, :, None]


def spread_heads(matrices, row_count, block_count, device_count):
    count = len(matrices)
    joined = jnp.stack(matrices).reshape(count, row_count, HEADS, HDIM)
    joined = jnp.transpose(joined, (2, 0, 1, 3)).reshape(HEADS, 1, count * row_count, HDIM)
    return jnp.broadcast_to(joined, (HEADS, block_count, count * row_count, HDIM)).reshape(
        device_count, count * row_count, HDIM
    )


def split_pieces(matrix, row_count, block_count, device_count):
    piece = row_count // block_count
    parted = matrix.reshape(block_count, piece, HEADS, HDIM)
    return jnp.transpose(parted, (2, 0, 1, 3)).reshape(device_count, piece, HDIM)


def local(query_src, key_src, value_src, up_query, query_gain, key_gain, up_gain):
    device_count = lax.axis_size("seq")
    device_index = lax.axis_index("seq")
    block_count = device_count // HEADS
    block_index = device_index % block_count
    token_count = query_src.shape[0]
    edges = jnp.stack(
        [
            query_src[token_count - SHIFT :],
            key_src[token_count - SHIFT :],
            value_src[token_count - SHIFT :],
        ]
    )
    edges = shifted(edges, "seq", 1)
    short_query = head_norm(pooled_rows(query_src, edges[0]), query_gain).astype(jnp.bfloat16)
    short_key = head_norm(pooled_rows(key_src, edges[1]), key_gain).astype(jnp.bfloat16)
    short_value = pooled_rows(value_src, edges[2]).astype(jnp.bfloat16)
    row_count = short_query.shape[0]
    up_heads = head_norm(up_query.astype(jnp.float32), up_gain).astype(jnp.bfloat16)
    row_total = row_count * device_count
    key_block = math.gcd(512, row_total)
    row_positions = jnp.arange(row_total, dtype=jnp.int32)
    device_rows = jnp.arange(device_count, dtype=jnp.int32)[:, None]
    qkv_out = spread_heads(
        [short_query, short_key, short_value], row_count, block_count, device_count
    )
    up_out = split_pieces(up_heads, token_count, block_count, device_count)
    arrived, own_up = (
        lax.all_to_all(qkv_out, "seq", split_axis=0, concat_axis=0, tiled=True),
        lax.all_to_all(up_out, "seq", split_axis=0, concat_axis=0, tiled=True),
    )
    all_query = arrived[:, :row_count].reshape(row_total, HDIM)
    all_key = arrived[:, row_count : 2 * row_count].reshape(row_total, HDIM)
    all_value = arrived[:, 2 * row_count :].reshape(row_total, HDIM)

    def fill_block(index_now, memory_now):
        offset = index_now * key_block
        block_query = lax.dynamic_slice_in_dim(all_query, offset, key_block, 0)[None]
        limits = offset + jnp.arange(key_block, dtype=jnp.int32)
        attended = blocked_attention(
            block_query, limits, all_key[None], all_value[None], row_positions, key_block
        )[0]
        return lax.dynamic_update_slice_in_dim(
            memory_now, row_norm(attended).astype(jnp.bfloat16), offset, 0
        )

    memory = lax.fori_loop(
        0, row_total // key_block, fill_block, jnp.zeros((row_total, HDIM), jnp.bfloat16)
    )
    token_piece = token_count // block_count
    own_tokens = (
        device_rows * token_count
        + block_index * token_piece
        + jnp.arange(token_piece, dtype=jnp.int32)[None, :]
    ).reshape(-1)
    own_up = own_up.reshape(1, device_count * token_piece, HDIM)
    result = blocked_attention(
        own_up, own_tokens // SHORT, memory[None], memory[None], row_positions, key_block
    )[0]
    result = result.astype(jnp.bfloat16).reshape(device_count, token_piece, HDIM)
    returned = lax.all_to_all(result, "seq", split_axis=0, concat_axis=0, tiled=True)
    output_heads = returned.reshape(HEADS, token_count, HDIM)
    return jnp.transpose(output_heads, (1, 0, 2)).reshape(token_count, HEADS * HDIM)


def solution(mesh):
    in_specs = (
        P(("groups", "seq"), None),
        P(("groups", "seq"), None),
        P(("groups", "seq"), None),
        P(("groups", "seq"), None),
        P(),
        P(),
        P(),
    )
    out_specs = P(("groups", "seq"), None)
    return jax.shard_map(local, mesh=mesh, in_specs=in_specs, out_specs=out_specs, check_vma=False)
```

profile of v0, /device:TPU:0, one launch (start us, length us, event | category | flops | bytes accessed | tf_op | source)
XLA Modules:
  0.0 73.4 jit_solution(4951900636859663489)
XLA Ops:
  0.0 0.8 %slice_bitcast_fusion.5 = bf16[1,3,2048]{2,1,0:T(4,128)(2,1)S(1)} fusion(bf16[128,2048]{1,0:T(8,128)(2,1)} %param.9), kind=kLoop, calls=%fused_computation.47 | loop fusion | bytes 24576 | tf_op jit(solution)/shard_map/stack | solution.py:101
  0.8 0.8 %slice_bitcast_fusion.3 = (bf16[1,3,2048]{2,1,0:T(4,128)(2,1)S(1)}, bf16[1,3,2048]{2,1,0:T(4,128)(2,1)S(1)}) fusion(bf16[128,2048]{1,0:T(8,128)(2,1)} %param.11, bf16[128,2048]{1,0:T(8,128)(2,1)} %param.10), kind=kLoop, calls=%fused_computation.45 | loop fusion | bytes 49152 | tf_op jit(solution)/shard_map/stack | solution.py:101
  1.6 2.4 %collective-permute-start = (bf16[3,3,2048]{2,1,0:T(4,128)(2,1)S(1)}, bf16[3,3,2048]{2,1,0:T(4,128)(2,1)S(1)}, u32[]{:S(2)}, u32[]{:S(2)}) collective-permute-start(bf16[3,3,2048]{2,1,0:T(4,128)(2,1)S(1)} %pad_maximum_fusion.1), channel_id=1, source_target_pairs={{0,1},{1,2},{2,3},{3,4},{4,5},{5,6},{6,7},{7,8},{8,9},{9,10},{10,1... | collective-permute-start | bytes 110600 | tf_op jit(solution)/shard_map/ppermute | solution.py:20
  4.0 0.9 %collective-permute-done = bf16[3,3,2048]{2,1,0:T(4,128)(2,1)S(1)} collective-permute-done((bf16[3,3,2048]{2,1,0:T(4,128)(2,1)S(1)}, bf16[3,3,2048]{2,1,0:T(4,128)(2,1)S(1)}, u32[]{:S(2)}, u32[]{:S(2)}) %collective-permute-start) | collective-permute-done | bytes 36896 | tf_op jit(solution)/shard_map/ppermute | solution.py:20
  4.9 1.2 %maximum_convert_fusion = f32[128,2048]{1,0:T(8,128)S(1)} fusion(bf16[125,2048]{1,0:T(8,128)(2,1)} %bitcast.90, bf16[3,2048]{1,0:T(4,128)(2,1)S(1)} %get-tuple-element.347), kind=kLoop, calls=%fused_computation.22 | loop fusion | flops 1048576 | bytes 1572864 | tf_op jit(solution)/shard_map/convert_element_type | solution.py:37
  6.1 0.3 reshape.261
  6.4 0.0 copy-start
  6.4 0.6 reduce_sum.89
  7.2 0.1 reduce_sum.91
  7.3 0.1 copy-done
  7.4 0.1 maximum_convert_fusion.2
  7.6 0.0 copy-start.1
  7.6 0.3 reshape.263
  7.9 0.6 reduce_sum.95
  8.6 0.0 copy-done.1
  8.6 0.1 maximum_convert_fusion.1
  8.8 0.3 reshape.262
  9.1 0.0 copy-start.4
  9.1 0.0 copy-start.5
  9.1 0.6 reduce_sum.92
  9.8 0.0 copy-start.2
  9.9 0.1 reduce_sum.94
  10.0 0.0 copy-done.4
  10.1 0.1 fusion.12
  10.2 0.0 copy-done.5
  10.2 0.0 copy-start.3
  10.2 0.1 fusion.10
  10.4 0.8 %copy.30 = bf16[16,96,128]{2,1,0:T(8,128)(2,1)} copy(bf16[16,96,128]{2,0,1:T(8,128)(2,1)S(1)} %bitcast.85) | data formatting | bytes 786432 | tf_op jit(solution)/shard_map/reshape;reshape | solution.py:84
  11.3 9.5 %all-to-all-start.1 = ((bf16[16,96,128]{2,1,0:T(8,128)(2,1)}), bf16[16,96,128]{2,1,0:T(8,128)(2,1)S(1)}, u32[]{:S(2)}, u32[]{:S(2)}) async-start(bf16[16,96,128]{2,1,0:T(8,128)(2,1)} %copy.30), calls=%async_computation.1 | async-start | bytes 786432 | tf_op jit(solution)/shard_map/all_to_all | solution.py:123
  20.8 0.7 fusion.16
  22.2 0.0 copy-done.2
  22.2 0.3 copy.29
  22.5 0.1 bitcast_reduce_fusion
  22.6 0.0 copy-done.3
  22.6 1.1 %fusion.7 = bf16[128,2048]{0,1:T(8,128)(2,1)} fusion(bf16[128,2048]{0,1:T(8,128)(2,1)S(1)} %copy.29, f32[2048]{0:T(1024)S(1)} %copy-done.3, f32[128,16]{0,1:T(8,128)S(1)} %add_rsqrt_fusion), kind=kLoop, calls=%fused_computation.18 | loop fusion | flops 1048576 | bytes 1064960 | tf_op jit(solution)/shard_map/convert_element_type | solution.py:113
  23.7 0.1 broadcast_in_dim.17
  23.8 9.2 %all-to-all-done.1 = bf16[16,96,128]{2,1,0:T(8,128)(2,1)S(1)} async-done(((bf16[16,96,128]{2,1,0:T(8,128)(2,1)}), bf16[16,96,128]{2,1,0:T(8,128)(2,1)S(1)}, u32[]{:S(2)}, u32[]{:S(2)}) %all-to-all-start.1) | async-done | bytes 393248 | tf_op jit(solution)/shard_map/all_to_all | solution.py:123
  33.0 3.6 %all-to-all-start = ((bf16[16,128,128]{1,2,0:T(8,128)(2,1)}), bf16[16,128,128]{1,2,0:T(8,128)(2,1)S(1)}, u32[]{:S(2)}, u32[]{:S(2)}) async-start(bf16[16,128,128]{1,2,0:T(8,128)(2,1)} %bitcast.5), calls=%async_computation | async-start | bytes 1048576 | tf_op jit(solution)/shard_map/all_to_all | solution.py:124
  36.6 0.3 fusion.21
  36.9 0.3 multiply_reduce_fusion
  37.3 13.7 %all-to-all-done = bf16[16,128,128]{1,2,0:T(8,128)(2,1)S(1)} async-done(((bf16[16,128,128]{1,2,0:T(8,128)(2,1)}), bf16[16,128,128]{1,2,0:T(8,128)(2,1)S(1)}, u32[]{:S(2)}, u32[]{:S(2)}) %all-to-all-start) | async-done | bytes 524320 | tf_op jit(solution)/shard_map/all_to_all | solution.py:124
  51.0 2.4 %conditional.1 = ((f32[1,2048,128]{2,1,0:T(8,128)S(1)}, f32[1,2048]{1,0:T(1,128)S(1)})) conditional(s32[]{:T(128)} %convert_element_type.96, (f32[1,2048,128]{2,1,0:T(8,128)S(1)}, f32[1,2048]{1,0:T(1,128)S(1)}) %tuple.32, (s32[512]{0:T(512)S(1)}, s32[2048]{0:T(1024)S(1)}, s32[2048]{0:T(1024)S(1)}, s32[]{:T(128)}, ...), branch_computations={%region_9.0_spmd, %region_10.12_spmd.clone} | conditional | flops 542406656 | bytes 8194076 | solution.py:70
  51.0 0.3 copy.31
  51.3 1.2 %fusion.19 = (f32[2048]{0:T(1024)S(1)}, bf16[2048,512]{0,1:T(8,128)(2,1)S(1)}) fusion(bf16[2048,128]{1,0:T(8,128)(2,1)S(1)} %bitcast.93, bf16[512,128]{0,1:T(8,128)(2,1)S(1)} %get-tuple-element.339, s32[2048]{0:T(1024)S(1)} %add_select_fusion, s32[512]{0:T(512)S(1)} %get-tuple-element.279), kind=kOutput, calls=%fused_computation.62 | convolution fusion | flops 273676288 | bytes 2770944 | tf_op jit(solution)/shard_map/while/body/eval_jaxpr/cond/branch_1_fun/hqd,hkd->hqk/dot_general | solution.py:56
  52.5 0.9 %fusion = f32[1,2048,128]{2,1,0:T(8,128)S(1)} fusion(f32[1,2048,128]{2,1,0:T(8,128)S(1)} %get-tuple-element.278, bf16[512,128]{0,1:T(8,128)(2,1)S(1)} %get-tuple-element.339, bf16[2048,512]{0,1:T(8,128)(2,1)S(1)} %get-tuple-element.343), kind=kOutput, calls=%fused_computation.2 | convolution fusion | flops 268697600 | bytes 4325376 | tf_op jit(solution)/shard_map/while/body/eval_jaxpr/cond/branch_1_fun/hqk,hkd->hqd/dot_general | solution.py:62
  53.4 0.3 divide_convert_fusion
  53.8 18.4 %all_to_all.15 = bf16[16,128,128]{2,1,0:T(8,128)(2,1)S(1)} all-to-all(bf16[16,128,128]{2,1,0:T(8,128)(2,1)S(1)} %bitcast.83), channel_id=1, replica_groups=mesh['groups'=2,'seq'=16] {'seq'}, dimensions={0} | all-to-all | bytes 1048576 | tf_op jit(solution)/shard_map/all_to_all | solution.py:155
  72.1 0.3 copy.33
  72.4 1.0 %copy.34 = bf16[128,2048]{1,0:T(8,128)(2,1)} copy(bf16[128,2048]{0,1:T(8,128)(2,1)S(1)} %bitcast.84) | data formatting | bytes 1048576 | tf_op jit(solution)/shard_map/reshape | solution.py:157
  (22 shorter events, 0.5 us)
Async XLA Ops:
  1.6 3.2 %collective-permute-start = (bf16[3,3,2048]{2,1,0:T(4,128)(2,1)S(1)}, bf16[3,3,2048]{2,1,0:T(4,128)(2,1)S(1)}, u32[]{:S(2)}, u32[]{:S(2)}) collective-permute-start(bf16[3,3,2048]{2,1,0:T(4,128)(2,1)S(1)} %pad_maximum_fusion.1), channel_id=1, source_target_pairs={{0,1},{1,2},{2,3},{3,4},{4,5},{5,6},{6,7},{7,8},{8,9},{9,10},{10,1... | collective-permute-start | bytes 110600 | tf_op jit(solution)/shard_map/ppermute | solution.py:20
  6.4 1.0 %copy-start = (bf16[128,2048]{1,0:T(8,128)(2,1)S(1)}, bf16[128,2048]{1,0:T(8,128)(2,1)}, u32[]{:S(2)}) copy-start(bf16[128,2048]{1,0:T(8,128)(2,1)} %param.11) | copy-start | bytes 1572868
  7.6 1.0 %copy-start.1 = (bf16[128,2048]{1,0:T(8,128)(2,1)S(1)}, bf16[128,2048]{1,0:T(8,128)(2,1)}, u32[]{:S(2)}) copy-start(bf16[128,2048]{1,0:T(8,128)(2,1)} %param.10) | copy-start | bytes 1572868
  9.1 1.0 %copy-start.4 = (f32[2048]{0:T(1024)S(1)}, f32[2048]{0:T(1024)}, u32[]{:S(2)}) copy-start(f32[2048]{0:T(1024)} %param.13) | copy-start | bytes 24580
  9.1 1.1 %copy-start.5 = (f32[2048]{0:T(1024)S(1)}, f32[2048]{0:T(1024)}, u32[]{:S(2)}) copy-start(f32[2048]{0:T(1024)} %param.14) | copy-start | bytes 24580
  9.8 12.4 %copy-start.2 = (bf16[128,2048]{1,0:T(8,128)(2,1)S(1)}, bf16[128,2048]{1,0:T(8,128)(2,1)}, u32[]{:S(2)}) copy-start(bf16[128,2048]{1,0:T(8,128)(2,1)} %param.12) | copy-start | bytes 1572868
  10.2 12.4 %copy-start.3 = (f32[2048]{0:T(1024)S(1)}, f32[2048]{0:T(1024)}, u32[]{:S(2)}) copy-start(f32[2048]{0:T(1024)} %param.15) | copy-start | bytes 24580
  11.3 21.7 %all-to-all-start.1 = ((bf16[16,96,128]{2,1,0:T(8,128)(2,1)}), bf16[16,96,128]{2,1,0:T(8,128)(2,1)S(1)}, u32[]{:S(2)}, u32[]{:S(2)}) async-start(bf16[16,96,128]{2,1,0:T(8,128)(2,1)} %copy.30), calls=%async_computation.1 | async-start | bytes 786432 | tf_op jit(solution)/shard_map/all_to_all | solution.py:123
  33.0 18.0 %all-to-all-start = ((bf16[16,128,128]{1,2,0:T(8,128)(2,1)}), bf16[16,128,128]{1,2,0:T(8,128)(2,1)S(1)}, u32[]{:S(2)}, u32[]{:S(2)}) async-start(bf16[16,128,128]{1,2,0:T(8,128)(2,1)} %bitcast.5), calls=%async_computation | async-start | bytes 1048576 | tf_op jit(solution)/shard_map/all_to_all | solution.py:124
where the time goes:
time: 74.1 us; the launch traced here: 73.4 us
  waiting for transfers between devices  23.8 us (32%)
  blocking collectives  18.4 us (25%)
  starting transfers between devices  15.5 us (21%)
  other arithmetic  6.43 us (9%)
  local copies, waits for them, and re-layouts  5.64 us (8%)
  matrix products  2.67 us (4%)
  between operations  1.04 us (1%)
    all_to_all x1, blocking collectives, local(): lax.all_to_all(result, 'seq', split_axis=0, concat_axis=0, tiled=True)  18.4 us
    all_to_all x1, waiting for transfers between devices, local(): lax.all_to_all(up_out, 'seq', split_axis=0, concat_axis=0, tiled=True)  13.7 us
    all_to_all x1, starting transfers between devices, local(): lax.all_to_all(qkv_out, 'seq', split_axis=0, concat_axis=0, tiled=True)  9.54 us
    all_to_all x1, waiting for transfers between devices, local(): lax.all_to_all(qkv_out, 'seq', split_axis=0, concat_axis=0, tiled=True)  9.18 us
    all_to_all x1, starting transfers between devices, local(): lax.all_to_all(up_out, 'seq', split_axis=0, concat_axis=0, tiled=True)  3.57 us
    ppermute x1, starting transfers between devices, shifted(): lax.ppermute(value, axis, [(source, source + steps) for source in range(l...  2.36 us
    reduce_sum x3, other arithmetic, pooled_rows(): return jnp.mean(widened.reshape(-1, SHORT, widened.shape[1]), axis=1)  1.9 us
    another operation x2, local copies, waits for them, and re-layouts, local(): jnp.stack([query_src[token_count - SHIFT:], key_src[token_count - SHIFT:]...  1.57 us
  transfers between devices with their start and end apart: 3, of which 3 were waited for; matrix products, arithmetic and copies ran while one was open for 4% of the time, Pallas kernels for 0%

commit v1 on v0

--- a/solution.py
+++ b/solution.py
@@ -1,8 +1,11 @@
+import functools
 import math
 
 import jax
 import jax.numpy as jnp
 from jax import lax
+from jax.experimental import pallas as pl
+from jax.experimental.pallas import tpu as pltpu
 from jax.sharding import PartitionSpec as P
 
 HEADS = 16
@@ -92,7 +95,7 @@
     return jnp.transpose(parted, (2, 0, 1, 3)).reshape(device_count, piece, HDIM)
 
 
-def local(query_src, key_src, value_src, up_query, query_gain, key_gain, up_gain):
+def local_general(query_src, key_src, value_src, up_query, query_gain, key_gain, up_gain):
     device_count = lax.axis_size("seq")
     device_index = lax.axis_index("seq")
     block_count = device_count // HEADS
@@ -157,6 +160,308 @@
     return jnp.transpose(output_heads, (1, 0, 2)).reshape(token_count, HEADS * HDIM)
 
 
+NT = (((1,), (1,)), ((), ()))
+
+
+def attend(queries, keys, values, first_row, tokens_per_row, masked_from):
+    scores = lax.dot_general(queries, keys, NT, preferred_element_type=jnp.float32)
+    exponent = jnp.exp(scores * (1.0 / math.sqrt(HDIM)))
+    last = exponent[:, masked_from:]
+    row = lax.broadcasted_iota(jnp.int32, last.shape, 0) + first_row
+    key = lax.broadcasted_iota(jnp.int32, last.shape, 1) * tokens_per_row
+    last = jnp.where(key <= row, last, 0.0)
+    parts = [last]
+    if masked_from:
+        parts = [exponent[:, :masked_from], last]
+    exponent = jnp.concatenate(parts, axis=1) if masked_from else last
+    denominator = jnp.sum(exponent, axis=1, keepdims=True)
+    numerator = jnp.dot(
+        exponent.astype(jnp.bfloat16), values, preferred_element_type=jnp.float32
+    )
+    return numerator / denominator
+
+
+def fused_kernel(
+    n, team, planes,
+    query_src, key_src, value_src, up_query, query_gain, key_gain, up_gain,
+    out_ref,
+    edge_send, edge_recv, up_send, up_recv, qkv_send, qkv_recv, mem, ret_send,
+    edge_sems, up_ssem, up_rsem, qkv_ssem, qkv_rsem, mem_ssem, mem_rsem, ret_ssem, ret_rsem,
+    local_sems,
+):
+    me = lax.axis_index("seq")
+    plane = me // team
+    member = me % team
+    tokens = query_src.shape[0]
+    rows = tokens // SHORT
+    block = rows * team
+
+    def remote(src, dst, ssem, rsem, target):
+        return pltpu.make_async_remote_copy(
+            src_ref=src, dst_ref=dst, send_sem=ssem, recv_sem=rsem,
+            device_id={"seq": target}, device_id_type=pl.DeviceIdType.MESH,
+        )
+
+    barrier = pltpu.get_barrier_semaphore()
+
+    @pl.loop(1, n)
+    def _(k):
+        pl.semaphore_signal(
+            barrier, inc=1, device_id={"seq": (me + k) % n},
+            device_id_type=pl.DeviceIdType.MESH,
+        )
+
+    sources = (query_src, key_src, value_src)
+    edge_token = lax.broadcasted_iota(jnp.int32, (8, tokens), 1)
+    edge_row = lax.broadcasted_iota(jnp.int32, (8, tokens), 0)
+    edge = None
+    for at, source in enumerate(sources):
+        pick = jnp.where(
+            (edge_row == at) & (edge_token >= tokens - SHIFT), 1.0 / SHORT, 0.0
+        ).astype(jnp.bfloat16)
+        term = jnp.dot(pick, source[...], preferred_element_type=jnp.float32)
+        edge = term if edge is None else edge + term
+    edge_send[...] = edge
+    pl.semaphore_wait(barrier, n - 1)
+
+    edge_copy = remote(
+        edge_send, edge_recv, edge_sems.at[0], edge_sems.at[1], lax.min(me + 1, n - 1)
+    )
+
+    @pl.when(me < n - 1)
+    def _():
+        edge_copy.start()
+
+    for head in range(HEADS):
+        cols = slice(head * HDIM, (head + 1) * HDIM)
+        part = up_query[:, cols].astype(jnp.float32)
+        scale = lax.rsqrt(jnp.mean(part * part, axis=1, keepdims=True) + epsilon)
+        up_send[head] = (part * scale * up_gain[:, cols]).astype(jnp.bfloat16)
+
+    edge_recv_zero = me == 0
+
+    @pl.when(edge_recv_zero)
+    def _():
+        edge_recv[...] = jnp.zeros_like(edge_recv)
+
+    @pl.when(me > 0)
+    def _():
+        edge_copy.wait_recv()
+
+    pool_row = lax.broadcasted_iota(jnp.int32, (rows, tokens), 0) * SHORT
+    pool_token = lax.broadcasted_iota(jnp.int32, (rows, tokens), 1)
+    pool = jnp.where(
+        (pool_token <= pool_row) & (pool_token >= pool_row - SHIFT), 1.0 / SHORT, 0.0
+    ).astype(jnp.bfloat16)
+    first = lax.broadcasted_iota(jnp.int32, (rows, HDIM), 0) == 0
+    for at, (source, gain) in enumerate(zip(sources, (query_gain, key_gain, None))):
+        pooled = jnp.dot(pool, source[...], preferred_element_type=jnp.float32)
+        for head in range(HEADS):
+            cols = slice(head * HDIM, (head + 1) * HDIM)
+            part = pooled[:, cols]
+            part = part + jnp.where(first, edge_recv[at : at + 1, cols], 0.0)
+            if gain is not None:
+                scale = lax.rsqrt(jnp.mean(part * part, axis=1, keepdims=True) + epsilon)
+                part = part * scale * gain[:, cols]
+            qkv_send[head, at * rows : (at + 1) * rows] = part.astype(jnp.bfloat16)
+
+    def head_of(device):
+        return (device % team) * planes + device // team
+
+    def qkv_copy(target):
+        return remote(
+            qkv_send.at[head_of(target)], qkv_recv.at[me],
+            qkv_ssem.at[target], qkv_rsem.at[me], target,
+        )
+
+    @pl.loop(1, n)
+    def _(k):
+        qkv_copy((me + k) % n).start()
+
+    def up_copy(target):
+        return remote(
+            up_send.at[pl.ds(target * planes, planes)], up_recv.at[member],
+            up_ssem.at[target], up_rsem.at[member], plane * team + target,
+        )
+
+    @pl.loop(1, team)
+    def _(k):
+        up_copy((member + k) % team).start()
+
+    own_qkv = pltpu.make_async_copy(
+        qkv_send.at[head_of(me)], qkv_recv.at[me], local_sems.at[0]
+    )
+    own_up = pltpu.make_async_copy(
+        up_send.at[pl.ds(member * planes, planes)], up_recv.at[member], local_sems.at[1]
+    )
+    own_qkv.start()
+    own_up.start()
+    own_qkv.wait()
+
+    def mem_copy(target, at):
+        part = mem.at[plane, at * block : (at + 1) * block]
+        return remote(
+            part, part, mem_ssem.at[target, at], mem_rsem.at[plane, at],
+            target * team + member,
+        )
+
+    for at in range(planes):
+        for other in range(team):
+            source = at * team + other
+
+            @pl.when(source != me)
+            def _():
+                remote(
+                    qkv_send.at[0], qkv_recv.at[source],
+                    qkv_ssem.at[source], qkv_rsem.at[source], source,
+                ).wait_recv()
+
+        upto = (at + 1) * team
+        queries = qkv_recv[at * team : upto, :rows].reshape(block, HDIM)
+        keys = qkv_recv[:upto, rows : 2 * rows].reshape(upto * rows, HDIM)
+        values = qkv_recv[:upto, 2 * rows :].reshape(upto * rows, HDIM)
+        attended = attend(queries, keys, values, 0, 1, at * block)
+        mem[plane, at * block : (at + 1) * block] = row_norm(attended).astype(jnp.bfloat16)
+        for target in reversed(range(at, planes)):
+
+            @pl.when(target != plane)
+            def _():
+                mem_copy(target, at).start()
+
+    own_up.wait()
+
+    @pl.loop(1, team)
+    def _(k):
+        source = (member + k) % team
+        remote(
+            up_send.at[pl.ds(0, planes)], up_recv.at[source],
+            up_ssem.at[source], up_rsem.at[source], plane * team + source,
+        ).wait_recv()
+
+    def ret_copy(target, part):
+        column = pl.multiple_of((member * planes + part) * HDIM, HDIM)
+        return remote(
+            ret_send.at[target, part], out_ref.at[:, pl.ds(column, HDIM)],
+            ret_ssem.at[target, part], ret_rsem.at[member, part], plane * team + target,
+        )
+
+    for here in range(planes):
+
+        @pl.when(plane == here)
+        def _():
+            count = (here + 1) * block
+
+            @pl.loop(0, planes)
+            def _(step):
+                part = (here + step) % planes
+
+                @pl.when(part != here)
+                def _():
+                    for at in range(here + 1):
+                        slot = mem.at[part, at * block : (at + 1) * block]
+                        remote(
+                            slot, slot, mem_ssem.at[part, at], mem_rsem.at[part, at],
+                            part * team + member,
+                        ).wait_recv()
+
+                memory = mem[part, :count]
+                for target in range(team):
+                    value = attend(
+                        up_recv[target, part], memory, memory,
+                        target * tokens, SHORT, here * block,
+                    ).astype(jnp.bfloat16)
+                    ret_send[target, part] = value
+
+                for target in range(team):
+
+                    @pl.when(target != member)
+                    def _():
+                        ret_copy(target, part).start()
+
+                column = pl.multiple_of((member * planes + part) * HDIM, HDIM)
+                out_ref[:, pl.ds(column, HDIM)] = ret_send[member, part]
+
+    @pl.when(me < n - 1)
+    def _():
+        edge_copy.wait_send()
+
+    @pl.loop(1, n)
+    def _(k):
+        qkv_copy((me + k) % n).wait_send()
+
+    @pl.loop(1, team)
+    def _(k):
+        up_copy((member + k) % team).wait_send()
+
+    for at in range(planes):
+        for target in range(at, planes):
+
+            @pl.when(target != plane)
+            def _():
+                mem_copy(target, at).wait_send()
+
+    @pl.loop(1, team)
+    def _(k):
+        other = (member + k) % team
+        for part in range(planes):
+            ret_copy(other, part).wait_send()
+            column = pl.multiple_of((other * planes + part) * HDIM, HDIM)
+            remote(
+                ret_send.at[other, part], out_ref.at[:, pl.ds(column, HDIM)],
+                ret_ssem.at[other, part], ret_rsem.at[other, part], plane * team + other,
+            ).wait_recv()
+
+
+def local_fused(query_src, key_src, value_src, up_query, query_gain, key_gain, up_gain):
+    n = lax.axis_size("seq")
+    team = math.isqrt(n)
+    planes = n // team
+    tokens, width = query_src.shape
+    rows = tokens // SHORT
+    bf16, dma = jnp.bfloat16, pltpu.SemaphoreType.DMA
+    return pl.pallas_call(
+        functools.partial(fused_kernel, n, team, planes),
+        out_shape=jax.ShapeDtypeStruct((tokens, width), bf16),
+        in_specs=[pl.BlockSpec(memory_space=pltpu.VMEM)] * 7,
+        out_specs=pl.BlockSpec(memory_space=pltpu.VMEM),
+        scratch_shapes=[
+            pltpu.VMEM((8, width), jnp.float32),
+            pltpu.VMEM((8, width), jnp.float32),
+            pltpu.VMEM((HEADS, tokens, HDIM), bf16),
+            pltpu.VMEM((team, planes, tokens, HDIM), bf16),
+            pltpu.VMEM((HEADS, 3 * rows, HDIM), bf16),
+            pltpu.VMEM((n, 3 * rows, HDIM), bf16),
+            pltpu.VMEM((planes, n * rows, HDIM), bf16),
+            pltpu.VMEM((team, planes, tokens, HDIM), bf16),
+            dma((2,)),
+            dma((team,)),
+            dma((team,)),
+            dma((n,)),
+            dma((n,)),
+            dma((planes, planes)),
+            dma((planes, planes)),
+            dma((team, planes)),
+            dma((team, planes)),
+            dma((2,)),
+        ],
+        compiler_params=pltpu.CompilerParams(
+            collective_id=0, has_side_effects=True, vmem_limit_bytes=48 * 1024 * 1024
+        ),
+    )(
+        query_src, key_src, value_src, up_query,
+        query_gain.reshape(1, width), key_gain.reshape(1, width), up_gain.reshape(1, width),
+    )
+
+
+def local(query_src, *others):
+    n = lax.axis_size("seq")
+    square = math.isqrt(n) ** 2 == n
+    whole_tiles = query_src.shape[0] % (16 * SHORT) == 0
+    if n == HEADS and square and whole_tiles:
+        return local_fused(query_src, *others)
+    return local_general(query_src, *others)
+
+
 def solution(mesh):
     in_specs = (
         P(("groups", "seq"), None),

time: 74.1 us -> 42.6 us (0.57)
  the two profiles are of different devices: /device:TPU:0 before, /device:TPU:17 now
where the time goes in v1:
time: 42.6 us; the launch traced here: 42.2 us
  Pallas kernels  35.1 us (82%)
  local copies, waits for them, and re-layouts  7.05 us (17%)
    pallas_call x1, Pallas kernels, local_fused(): pl.pallas_call(functools.partial(fused_kernel, n, team, planes), out_shap...  35.1 us
    unnamed x15, local copies, waits for them, and re-layouts  7.05 us

profile of v1, /device:TPU:17, one launch (start us, length us, event | category | flops | bytes accessed | tf_op | source)
XLA Modules:
  0.0 42.2 jit_solution(10717749617172840483)
XLA Ops:
  0.0 0.0 copy-start
  0.0 1.0 %copy-done = bf16[128,2048]{1,0:T(8,128)(2,1)S(1)} copy-done((bf16[128,2048]{1,0:T(8,128)(2,1)S(1)}, bf16[128,2048]{1,0:T(8,128)(2,1)}, u32[]{:S(2)}) %copy-start) | copy-done | bytes 524312
  1.0 0.0 copy-start.1
  1.0 1.0 %copy-done.1 = bf16[128,2048]{1,0:T(8,128)(2,1)S(1)} copy-done((bf16[128,2048]{1,0:T(8,128)(2,1)S(1)}, bf16[128,2048]{1,0:T(8,128)(2,1)}, u32[]{:S(2)}) %copy-start.1) | copy-done | bytes 524312
  2.1 0.0 copy-start.2
  2.1 1.0 %copy-done.2 = bf16[128,2048]{1,0:T(8,128)(2,1)S(1)} copy-done((bf16[128,2048]{1,0:T(8,128)(2,1)S(1)}, bf16[128,2048]{1,0:T(8,128)(2,1)}, u32[]{:S(2)}) %copy-start.2) | copy-done | bytes 524312
  3.1 0.0 copy-start.3
  3.1 1.0 %copy-done.3 = bf16[128,2048]{1,0:T(8,128)(2,1)S(1)} copy-done((bf16[128,2048]{1,0:T(8,128)(2,1)S(1)}, bf16[128,2048]{1,0:T(8,128)(2,1)}, u32[]{:S(2)}) %copy-start.3) | copy-done | bytes 524312
  4.2 0.0 copy-start.4
  4.2 0.7 %copy-done.4 = f32[2048]{0:T(1024)S(1)} copy-done((f32[2048]{0:T(1024)S(1)}, f32[2048]{0:T(1024)}, u32[]{:S(2)}) %copy-start.4) | copy-done | bytes 8216
  4.9 0.0 copy-start.5
  4.9 0.7 %copy-done.5 = f32[2048]{0:T(1024)S(1)} copy-done((f32[2048]{0:T(1024)S(1)}, f32[2048]{0:T(1024)}, u32[]{:S(2)}) %copy-start.5) | copy-done | bytes 8216
  5.6 0.0 copy-start.6
  5.6 0.7 %copy-done.6 = f32[2048]{0:T(1024)S(1)} copy-done((f32[2048]{0:T(1024)S(1)}, f32[2048]{0:T(1024)}, u32[]{:S(2)}) %copy-start.6) | copy-done | bytes 8216
  6.3 35.1 %shard_map.73 = bf16[128,2048]{1,0:T(8,128)(2,1)S(1)} custom-call(bf16[128,2048]{1,0:T(8,128)(2,1)S(1)} %copy-done, bf16[128,2048]{1,0:T(8,128)(2,1)S(1)} %copy-done.1, bf16[128,2048]{1,0:T(8,128)(2,1)S(1)} %copy-done.2, bf16[128,2048]{1,0:T(8,128)(2,1)S(1)} %copy-done.3, f32[1,2048]{1,0:T(1,128)S(1)} %bitcast.3, f32[1,2048]{1,0:T(1,128)S(1)} %bitcast.4, ...), custom_call_target="tpu_custom_call" | custom-call | tf_op jit(solution)/shard_map/pallas_call | solution.py:422
  41.4 0.8 %copy.9 = bf16[128,2048]{1,0:T(8,128)(2,1)} copy(bf16[128,2048]{1,0:T(8,128)(2,1)S(1)} %shard_map.73) | data formatting | bytes 1048576
Async XLA Ops:
  0.0 1.0 %copy-start = (bf16[128,2048]{1,0:T(8,128)(2,1)S(1)}, bf16[128,2048]{1,0:T(8,128)(2,1)}, u32[]{:S(2)}) copy-start(bf16[128,2048]{1,0:T(8,128)(2,1)} %query_src.1) | copy-start | bytes 1572868
  1.0 1.0 %copy-start.1 = (bf16[128,2048]{1,0:T(8,128)(2,1)S(1)}, bf16[128,2048]{1,0:T(8,128)(2,1)}, u32[]{:S(2)}) copy-start(bf16[128,2048]{1,0:T(8,128)(2,1)} %key_src.1) | copy-start | bytes 1572868
  2.1 1.0 %copy-start.2 = (bf16[128,2048]{1,0:T(8,128)(2,1)S(1)}, bf16[128,2048]{1,0:T(8,128)(2,1)}, u32[]{:S(2)}) copy-start(bf16[128,2048]{1,0:T(8,128)(2,1)} %value_src.1) | copy-start | bytes 1572868
  3.1 1.0 %copy-start.3 = (bf16[128,2048]{1,0:T(8,128)(2,1)S(1)}, bf16[128,2048]{1,0:T(8,128)(2,1)}, u32[]{:S(2)}) copy-start(bf16[128,2048]{1,0:T(8,128)(2,1)} %up_query.1) | copy-start | bytes 1572868
  4.2 0.7 %copy-start.4 = (f32[2048]{0:T(1024)S(1)}, f32[2048]{0:T(1024)}, u32[]{:S(2)}) copy-start(f32[2048]{0:T(1024)} %param.11) | copy-start | bytes 24580
  4.9 0.7 %copy-start.5 = (f32[2048]{0:T(1024)S(1)}, f32[2048]{0:T(1024)}, u32[]{:S(2)}) copy-start(f32[2048]{0:T(1024)} %param.12) | copy-start | bytes 24580
  5.6 0.7 %copy-start.6 = (f32[2048]{0:T(1024)S(1)}, f32[2048]{0:T(1024)}, u32[]{:S(2)}) copy-start(f32[2048]{0:T(1024)} %param.13) | copy-start | bytes 24580

commit v2 on v1

--- a/solution.py
+++ b/solution.py
@@ -183,11 +183,12 @@
 
 def fused_kernel(
     n, team, planes,
+    query_hbm, key_hbm, value_hbm, up_hbm, query_gain_hbm, key_gain_hbm, up_gain_hbm,
+    out_ref,
     query_src, key_src, value_src, up_query, query_gain, key_gain, up_gain,
-    out_ref,
     edge_send, edge_recv, up_send, up_recv, qkv_send, qkv_recv, mem, ret_send,
     edge_sems, up_ssem, up_rsem, qkv_ssem, qkv_rsem, mem_ssem, mem_rsem, ret_ssem, ret_rsem,
-    local_sems,
+    local_sems, in_sems,
 ):
     me = lax.axis_index("seq")
     plane = me // team
@@ -202,6 +203,16 @@
             device_id={"seq": target}, device_id_type=pl.DeviceIdType.MESH,
         )
 
+    loads = [
+        pltpu.make_async_copy(src, dst, in_sems.at[at])
+        for at, (src, dst) in enumerate((
+            (query_hbm, query_src), (key_hbm, key_src), (value_hbm, value_src),
+            (up_hbm, up_query), (query_gain_hbm, query_gain),
+            (key_gain_hbm, key_gain), (up_gain_hbm, up_gain),
+        ))
+    ]
+    for load in loads:
+        load.start()
     barrier = pltpu.get_barrier_semaphore()
 
     @pl.loop(1, n)
@@ -219,6 +230,7 @@
         pick = jnp.where(
             (edge_row == at) & (edge_token >= tokens - SHIFT), 1.0 / SHORT, 0.0
         ).astype(jnp.bfloat16)
+        loads[at].wait()
         term = jnp.dot(pick, source[...], preferred_element_type=jnp.float32)
         edge = term if edge is None else edge + term
     edge_send[...] = edge
@@ -232,37 +244,40 @@
     def _():
         edge_copy.start()
 
+    for load in loads[3:]:
+        load.wait()
     for head in range(HEADS):
         cols = slice(head * HDIM, (head + 1) * HDIM)
         part = up_query[:, cols].astype(jnp.float32)
         scale = lax.rsqrt(jnp.mean(part * part, axis=1, keepdims=True) + epsilon)
-        up_send[head] = (part * scale * up_gain[:, cols]).astype(jnp.bfloat16)
-
-    edge_recv_zero = me == 0
-
-    @pl.when(edge_recv_zero)
-    def _():
-        edge_recv[...] = jnp.zeros_like(edge_recv)
-
-    @pl.when(me > 0)
-    def _():
-        edge_copy.wait_recv()
+        up_send[head] = (part * scale * up_gain[head : head + 1]).astype(jnp.bfloat16)
 
     pool_row = lax.broadcasted_iota(jnp.int32, (rows, tokens), 0) * SHORT
     pool_token = lax.broadcasted_iota(jnp.int32, (rows, tokens), 1)
     pool = jnp.where(
         (pool_token <= pool_row) & (pool_token >= pool_row - SHIFT), 1.0 / SHORT, 0.0
     ).astype(jnp.bfloat16)
+    pooled_all = [
+        jnp.dot(pool, source[...], preferred_element_type=jnp.float32) for source in sources
+    ]
+
+    @pl.when(me == 0)
+    def _():
+        edge_recv[...] = jnp.zeros_like(edge_recv)
+
+    @pl.when(me > 0)
+    def _():
+        edge_copy.wait_recv()
+
     first = lax.broadcasted_iota(jnp.int32, (rows, HDIM), 0) == 0
-    for at, (source, gain) in enumerate(zip(sources, (query_gain, key_gain, None))):
-        pooled = jnp.dot(pool, source[...], preferred_element_type=jnp.float32)
+    for at, (pooled, gain) in enumerate(zip(pooled_all, (query_gain, key_gain, None))):
         for head in range(HEADS):
             cols = slice(head * HDIM, (head + 1) * HDIM)
             part = pooled[:, cols]
             part = part + jnp.where(first, edge_recv[at : at + 1, cols], 0.0)
             if gain is not None:
                 scale = lax.rsqrt(jnp.mean(part * part, axis=1, keepdims=True) + epsilon)
-                part = part * scale * gain[:, cols]
+                part = part * scale * gain[head : head + 1]
             qkv_send[head, at * rows : (at + 1) * rows] = part.astype(jnp.bfloat16)
 
     def head_of(device):
@@ -274,9 +289,16 @@
             qkv_ssem.at[target], qkv_rsem.at[me], target,
         )
 
-    @pl.loop(1, n)
-    def _(k):
-        qkv_copy((me + k) % n).start()
+    for hop in sorted(range(planes), key=lambda hop: -min(hop, planes - hop)):
+        target_plane = (plane + hop) % planes
+
+        @pl.loop(0, team)
+        def _(k):
+            target = target_plane * team + (member + k) % team
+
+            @pl.when(target != me)
+            def _():
+                qkv_copy(target).start()
 
     def up_copy(target):
         return remote(
@@ -422,9 +444,11 @@
     return pl.pallas_call(
         functools.partial(fused_kernel, n, team, planes),
         out_shape=jax.ShapeDtypeStruct((tokens, width), bf16),
-        in_specs=[pl.BlockSpec(memory_space=pltpu.VMEM)] * 7,
+        in_specs=[pl.BlockSpec(memory_space=pltpu.HBM)] * 7,
         out_specs=pl.BlockSpec(memory_space=pltpu.VMEM),
-        scratch_shapes=[
+        scratch_shapes=[pltpu.VMEM((tokens, width), bf16)] * 4
+        + [pltpu.VMEM((HEADS, HDIM), jnp.float32)] * 3
+        + [
             pltpu.VMEM((8, width), jnp.float32),
             pltpu.VMEM((8, width), jnp.float32),
             pltpu.VMEM((HEADS, tokens, HDIM), bf16),
@@ -443,13 +467,14 @@
             dma((team, planes)),
             dma((team, planes)),
             dma((2,)),
+            dma((7,)),
         ],
         compiler_params=pltpu.CompilerParams(
-            collective_id=0, has_side_effects=True, vmem_limit_bytes=48 * 1024 * 1024
+            collective_id=0, has_side_effects=True, vmem_limit_bytes=60 * 1024 * 1024
         ),
     )(
         query_src, key_src, value_src, up_query,
-        query_gain.reshape(1, width), key_gain.reshape(1, width), up_gain.reshape(1, width),
+        *(gain.reshape(HEADS, HDIM) for gain in (query_gain, key_gain, up_gain)),
     )
 
 

time: 42.6 us -> 34.7 us (0.81)
  the two profiles are of different devices: /device:TPU:17 before, /device:TPU:13 now
where the time goes in v2:
time: 34.7 us; the launch traced here: 34.5 us
  Pallas kernels  32.6 us (94%)
  local copies, waits for them, and re-layouts  1.88 us (5%)
    pallas_call x1, Pallas kernels, local_fused(): pl.pallas_call(functools.partial(fused_kernel, n, team, planes), out_shap...  32.6 us
    unnamed x1, local copies, waits for them, and re-layouts  1.88 us

profile of v2, /device:TPU:13, one launch (start us, length us, event | category | flops | bytes accessed | tf_op | source)
XLA Modules:
  0.0 34.5 jit_solution(1753027452120798358)
XLA Ops:
  0.0 32.6 %shard_map.73 = bf16[128,2048]{1,0:T(8,128)(2,1)} custom-call(bf16[128,2048]{1,0:T(8,128)(2,1)} %query_hbm.1, bf16[128,2048]{1,0:T(8,128)(2,1)} %key_hbm.1, bf16[128,2048]{1,0:T(8,128)(2,1)} %value_hbm.1, bf16[128,2048]{1,0:T(8,128)(2,1)} %up_hbm.1, f32[16,128]{1,0:T(8,128)} %bitcast.3, f32[16,128]{1,0:T(8,128)} %bitcast.4, f32[16,128]{1,0:T(8,128)} %bitcast.5), custom_call_target="tpu_custom_call" | custom-call | tf_op jit(solution)/shard_map/pallas_call | solution.py:444
  32.6 1.9 %copy.9 = bf16[128,2048]{1,0:T(8,128)(2,1)} copy(bf16[128,2048]{1,0:T(8,128)(2,1)} %shard_map.73) | data formatting | bytes 1048576

commit v3 on v2

--- a/solution.py
+++ b/solution.py
@@ -436,7 +436,7 @@
 
 def local_fused(query_src, key_src, value_src, up_query, query_gain, key_gain, up_gain):
     n = lax.axis_size("seq")
-    team = math.isqrt(n)
+    team = n // 2
     planes = n // team
     tokens, width = query_src.shape
     rows = tokens // SHORT
@@ -480,9 +480,9 @@
 
 def local(query_src, *others):
     n = lax.axis_size("seq")
-    square = math.isqrt(n) ** 2 == n
+    paired = n % 2 == 0
     whole_tiles = query_src.shape[0] % (16 * SHORT) == 0
-    if n == HEADS and square and whole_tiles:
+    if n == HEADS and paired and whole_tiles:
         return local_fused(query_src, *others)
     return local_general(query_src, *others)
 

time: 34.7 us -> 34 us (0.980)
  the two profiles are of different devices: /device:TPU:13 before, /device:TPU:0 now
where the time goes in v3:
time: 34 us; the launch traced here: 33.7 us
  Pallas kernels  31.8 us (94%)
  local copies, waits for them, and re-layouts  1.88 us (6%)
    pallas_call x1, Pallas kernels, local_fused(): pl.pallas_call(functools.partial(fused_kernel, n, team, planes), out_shap...  31.8 us
    unnamed x1, local copies, waits for them, and re-layouts  1.88 us

profile of v3, /device:TPU:0, one launch (start us, length us, event | category | flops | bytes accessed | tf_op | source)
XLA Modules:
  0.0 33.7 jit_solution(15901830814321038505)
XLA Ops:
  0.0 31.8 %shard_map.73 = bf16[128,2048]{1,0:T(8,128)(2,1)} custom-call(bf16[128,2048]{1,0:T(8,128)(2,1)} %query_hbm.1, bf16[128,2048]{1,0:T(8,128)(2,1)} %key_hbm.1, bf16[128,2048]{1,0:T(8,128)(2,1)} %value_hbm.1, bf16[128,2048]{1,0:T(8,128)(2,1)} %up_hbm.1, f32[16,128]{1,0:T(8,128)} %bitcast.3, f32[16,128]{1,0:T(8,128)} %bitcast.4, f32[16,128]{1,0:T(8,128)} %bitcast.5), custom_call_target="tpu_custom_call" | custom-call | tf_op jit(solution)/shard_map/pallas_call | solution.py:444
  31.8 1.9 %copy.9 = bf16[128,2048]{1,0:T(8,128)(2,1)} copy(bf16[128,2048]{1,0:T(8,128)(2,1)} %shard_map.73) | data formatting | bytes 1048576

commit v4 on v3

--- a/solution.py
+++ b/solution.py
@@ -387,21 +387,25 @@
                         ).wait_recv()
 
                 memory = mem[part, :count]
-                for target in range(team):
-                    value = attend(
-                        up_recv[target, part], memory, memory,
-                        target * tokens, SHORT, here * block,
-                    ).astype(jnp.bfloat16)
-                    ret_send[target, part] = value
-
-                for target in range(team):
-
-                    @pl.when(target != member)
-                    def _():
-                        ret_copy(target, part).start()
-
-                column = pl.multiple_of((member * planes + part) * HDIM, HDIM)
-                out_ref[:, pl.ds(column, HDIM)] = ret_send[member, part]
+                hops = sorted(range(team), key=lambda hop: -min(hop, team - hop))
+                for at in range(0, team, team // 2):
+                    targets = [(member + hop) % team for hop in hops[at : at + team // 2]]
+                    values = [
+                        attend(
+                            up_recv[target, part], memory, memory,
+                            target * tokens, SHORT, here * block,
+                        ).astype(jnp.bfloat16)
+                        for target in targets
+                    ]
+                    for hop, target, value in zip(hops[at:], targets, values):
+                        if hop:
+                            ret_send[target, part] = value
+                        else:
+                            column = pl.multiple_of((member * planes + part) * HDIM, HDIM)
+                            out_ref[:, pl.ds(column, HDIM)] = value
+                    for hop, target in zip(hops[at:], targets):
+                        if hop:
+                            ret_copy(target, part).start()
 
     @pl.when(me < n - 1)
     def _():

time: 34 us -> 34.5 us (1.015)
  Pallas kernels: 31.8 us -> 32.4 us
    pallas_call x1, Pallas kernels: 31.8 us -> 32.4 us  [local_fused(): pl.pallas_call(functools.partial(fused_kernel, n, team, planes), out_shap...]
where the time goes in v4:
time: 34.5 us; the launch traced here: 34.3 us
  Pallas kernels  32.4 us (94%)
  local copies, waits for them, and re-layouts  1.88 us (5%)
    pallas_call x1, Pallas kernels, local_fused(): pl.pallas_call(functools.partial(fused_kernel, n, team, planes), out_shap...  32.4 us
    unnamed x1, local copies, waits for them, and re-layouts  1.88 us

profile of v4, /device:TPU:0, one launch (start us, length us, event | category | flops | bytes accessed | tf_op | source)
XLA Modules:
  0.0 34.3 jit_solution(1238741072334841474)
XLA Ops:
  0.0 32.4 %shard_map.73 = bf16[128,2048]{1,0:T(8,128)(2,1)} custom-call(bf16[128,2048]{1,0:T(8,128)(2,1)} %query_hbm.1, bf16[128,2048]{1,0:T(8,128)(2,1)} %key_hbm.1, bf16[128,2048]{1,0:T(8,128)(2,1)} %value_hbm.1, bf16[128,2048]{1,0:T(8,128)(2,1)} %up_hbm.1, f32[16,128]{1,0:T(8,128)} %bitcast.3, f32[16,128]{1,0:T(8,128)} %bitcast.4, f32[16,128]{1,0:T(8,128)} %bitcast.5), custom_call_target="tpu_custom_call" | custom-call | tf_op jit(solution)/shard_map/pallas_call | solution.py:448
  32.4 1.9 %copy.9 = bf16[128,2048]{1,0:T(8,128)(2,1)} copy(bf16[128,2048]{1,0:T(8,128)(2,1)} %shard_map.73) | data formatting | bytes 1048576
